TPU v7x, 32 devices: a whole 2x2x4 slice. The times are simulated.
32 devices in a mesh: seq: 4 (over z), dp: 2 (over y), mp: 4 (over x, core).
Axes of the slice: x: 2, y: 2, z: 4, core: 2. Of those that a mesh axis runs over, the one named last changes fastest.
Arguments:
- features: bfloat16 [2, 1024, 8, 512], P('dp', 'seq', None, 'mp'), may hold values from -6 to 6
- key_projection: bfloat16 [2, 1024, 8, 128], P('dp', 'seq'), may hold values from -2 to 2
- query_proj: bfloat16 [2, 1024, 8, 128], P('dp', 'seq'), may hold values from -2 to 2
- step_raw: float32 [2, 1024, 8, 8], P('dp', 'seq', None, 'mp'), may hold values from -3 to 6
- doc_starts: int32 [2, 1024], P('dp', 'seq'), may hold values 0 or 1
- log_rate: float32 [8, 8], P(None, 'mp'), may hold values from -5 to 1
- step_bias: float32 [8, 8], P(None, 'mp'), may hold values from -5 to -2.5
- skip_gain: float32 [8, 8], P(None, 'mp'), may hold values from 0.5 to 1.5
- out_grad: bfloat16 [2, 1024, 8, 512], P('dp', 'seq', None, 'mp'), may hold values from -6 to 6
Outputs:
- mixed_out: bfloat16 [2, 1024, 8, 512], P('dp', 'seq', None, 'mp')
- features_grad: bfloat16 [2, 1024, 8, 512], P('dp', 'seq', None, 'mp')
- key_grad: bfloat16 [2, 1024, 8, 128], P('dp', 'seq', 'mp')
- query_grad: bfloat16 [2, 1024, 8, 128], P('dp', 'seq', 'mp')
- step_grad: float32 [2, 1024, 8, 8], P('dp', 'seq', None, 'mp')
- log_rate_grad: float32 [8, 8], P(None, 'mp')
- step_bias_grad: float32 [8, 8], P(None, 'mp')
- skip_grad: float32 [8, 8], P(None, 'mp')
All inputs are finite; a program needn't handle non-finite values. No bound on the sum of `doc_starts` on one device may be relied on, other than what follows from the above.
Results may differ from a plain program's by a relative error of at most 0.0015.
Values sent between devices are 32-bit elements; how exact they have to be, the bound alone decides.
A program may use at most 128 MiB of HBM per device.

v0:
```python
import math

import jax
import jax.numpy as jnp
from jax import lax
from jax.sharding import PartitionSpec as P

P_SIZE = 64


triple = lax.Precision.HIGH


def prefix(shard, axis, combine, identity):
    length, position = (lax.axis_size(axis), lax.axis_index(axis))
    everything = jax.tree.map(lambda part: lax.all_gather(part, axis), shard)
    start = jax.tree.map(
        lambda part, zero: jnp.broadcast_to(jnp.asarray(zero, part.dtype), part.shape),
        shard,
        identity,
    )

    def step(k, before):
        at = length - 1 - k
        reached = at > position
        new = combine(before, jax.tree.map(lambda part: part[at], everything))
        return jax.tree.map(lambda a, b: jnp.where(reached, a, b), new, before)

    return lax.fori_loop(0, length, step, start)


def decay_terms(step_raw, doc_starts, log_rate, step_bias):
    step_size = jax.nn.softplus(step_raw + step_bias)
    log_decay = -step_size * jnp.exp(log_rate)
    cumulative = jnp.cumsum(log_decay, axis=1)
    doc_count = jnp.cumsum(doc_starts, axis=1)
    return (step_size, cumulative, doc_count)


def block_forward(
    head_vals, key_vals, query_vals, step_raw, doc_starts, log_rate, step_bias, skip_gain, state_in
):
    step_size, cumulative, doc_count = decay_terms(step_raw, doc_starts, log_rate, step_bias)
    block_len = head_vals.shape[1]
    causal = jnp.arange(block_len)[:, None] >= jnp.arange(block_len)[None, :]
    same_doc = causal[None] & (doc_count[:, :, None] == doc_count[:, None, :])
    doc_mask = same_doc[..., None, None]
    gap_log = cumulative[:, :, None] - cumulative[:, None, :]
    decay_mat = jnp.where(doc_mask, jnp.exp(jnp.where(doc_mask, gap_log, 0.0)), 0.0)
    entry_decay = jnp.where((doc_count == 0)[:, :, None, None], jnp.exp(cumulative), 0.0)
    scores = jnp.einsum("rtgn,rsgn->rtsg", query_vals, key_vals, precision=triple)
    mixing = scores[..., None] * decay_mat * step_size[:, None]
    output = jnp.einsum("rtsgh,rsghp->rtghp", mixing, head_vals, precision=triple)
    output = (
        output
        + jnp.einsum("rtgn,rghpn->rtghp", query_vals, state_in, precision=triple)
        * entry_decay[..., None]
    )
    output = output + skip_gain[..., None] * head_vals
    last_decay = decay_mat[:, -1]
    state_out = state_in * entry_decay[:, -1][..., None, None]
    state_out = state_out + jnp.einsum(
        "rsgh,rsghp,rsgn->rghpn", last_decay * step_size, head_vals, key_vals, precision=triple
    )
    return (output, state_out)


def block_summary(head_vals, key_vals, step_raw, doc_starts, log_rate, step_bias):
    step_size, cumulative, doc_count = decay_terms(step_raw, doc_starts, log_rate, step_bias)
    tail_doc = (doc_count == doc_count[:, -1:])[:, :, None, None]
    last_decay = jnp.where(
        tail_doc, jnp.exp(jnp.where(tail_doc, cumulative[:, -1:] - cumulative, 0.0)), 0.0
    )
    passed_forward = jnp.where(
        (doc_count[:, -1] == 0)[:, None, None], jnp.exp(cumulative[:, -1]), 0.0
    )
    summary_state = jnp.einsum(
        "rsgh,rsghp,rsgn->rghpn", last_decay * step_size, head_vals, key_vals, precision=triple
    )
    return (passed_forward, summary_state)


def backward_combine(earlier, trailing_portion):
    return (
        earlier[0] * trailing_portion[0],
        trailing_portion[1] + trailing_portion[0][..., None, None] * earlier[1],
    )


def fold_states(passed_forward, summary_state):
    shard_count = lax.axis_size("seq")
    device_index = lax.axis_index("seq")
    row_count = passed_forward.shape[0]
    all_carried = lax.all_gather(passed_forward, "seq", axis=0, tiled=True)
    carry_table = all_carried.reshape((shard_count,) + passed_forward.shape)
    shard_ids = jnp.arange(shard_count)
    inside_run = (shard_ids[None, :] > shard_ids[:, None]) & (shard_ids[None, :] < device_index)
    factors = jnp.prod(
        jnp.where(inside_run[:, :, None, None, None], carry_table[None], 1.0), axis=1
    )
    weights = jnp.where((shard_ids < device_index)[:, None, None, None], factors, 0.0)
    weights = weights.reshape((shard_count * row_count,) + passed_forward.shape[1:])
    shard_piece = lax.all_gather(summary_state, "seq", axis=0, tiled=True)
    piece_rows = shard_piece.shape[0]
    row_select = (jnp.arange(piece_rows) % row_count)[:, None] == jnp.arange(row_count)[None, :]
    return jnp.einsum(
        "ir,igh,ighpn->rghpn",
        row_select.astype(jnp.float32),
        weights,
        shard_piece,
        precision=triple,
    )


def local(
    features,
    key_projection,
    query_proj,
    step_raw,
    doc_starts,
    log_rate,
    step_bias,
    skip_gain,
    out_grad,
):
    row_count, length, groups, feat_width = features.shape
    head_count = feat_width // P_SIZE
    block_len = math.gcd(length, 128)
    block_count = length // block_len
    head_vals = features.astype(jnp.float32).reshape(row_count, length, groups, head_count, P_SIZE)
    key_vals = key_projection.astype(jnp.float32)
    query_vals = query_proj.astype(jnp.float32)
    passed_forward, summary_state = block_summary(
        head_vals, key_vals, step_raw, doc_starts, log_rate, step_bias
    )
    state_in = fold_states(passed_forward, summary_state)

    def to_blocks(array):
        return jnp.moveaxis(
            array.reshape((row_count, block_count, block_len) + array.shape[2:]), 1, 0
        )

    def local_layer(
        head_vals, key_vals, query_vals, step_raw, log_rate, step_bias, skip_gain, state_in
    ):

        def stepper(state, pieces):
            vals_b, keys_b, queries_b, raw_b, starts_b = pieces
            output, new_state = block_forward(
                vals_b, keys_b, queries_b, raw_b, starts_b, log_rate, step_bias, skip_gain, state
            )
            return (new_state, output)

        final_state, block_outs = lax.scan(
            jax.checkpoint(stepper),
            state_in,
            (
                to_blocks(head_vals),
                to_blocks(key_vals),
                to_blocks(query_vals),
                to_blocks(step_raw),
                to_blocks(doc_starts),
            ),
        )
        outputs = jnp.moveaxis(block_outs, 0, 1).reshape(
            row_count, length, groups, head_count, P_SIZE
        )
        return (outputs, final_state)

    primal, pullback = jax.vjp(
        local_layer,
        head_vals,
        key_vals,
        query_vals,
        step_raw,
        log_rate,
        step_bias,
        skip_gain,
        state_in,
    )
    mixed_vals = primal[0]
    cotangent = out_grad.astype(jnp.float32).reshape(head_vals.shape)
    _, cumulative, doc_count = decay_terms(step_raw, doc_starts, log_rate, step_bias)
    entry_decay = jnp.where((doc_count == 0)[:, :, None, None], jnp.exp(cumulative), 0.0)
    adjoint_local = jnp.einsum(
        "rtgh,rtghp,rtgn->rghpn", entry_decay, cotangent, query_vals, precision=triple
    )
    adjoint_in = prefix(
        (passed_forward, adjoint_local),
        "seq",
        backward_combine,
        (jnp.ones_like(passed_forward), jnp.zeros_like(adjoint_local)),
    )[1]
    gradients = pullback((cotangent, adjoint_in))
    vals_grad, keys_grad, queries_grad, raw_grad, rate_grad, bias_grad, gain_grad, _ = gradients
    key_part, query_part = (
        lax.psum_scatter(keys_grad, "mp", scatter_dimension=2, tiled=True),
        lax.psum_scatter(queries_grad, "mp", scatter_dimension=2, tiled=True),
    )
    rate_total, bias_total, gain_total = lax.psum((rate_grad, bias_grad, gain_grad), ("seq", "dp"))
    return (
        mixed_vals.reshape(features.shape).astype(jnp.bfloat16),
        vals_grad.reshape(features.shape).astype(jnp.bfloat16),
        key_part.astype(jnp.bfloat16),
        query_part.astype(jnp.bfloat16),
        raw_grad,
        rate_total,
        bias_total,
        gain_total,
    )


def solution(mesh):
    return jax.shard_map(
        local,
        mesh=mesh,
        in_specs=(
            P("dp", "seq", None, "mp"),
            P("dp", "seq", None, None),
            P("dp", "seq", None, None),
            P("dp", "seq", None, "mp"),
            P("dp", "seq"),
            P(None, "mp"),
            P(None, "mp"),
            P(None, "mp"),
            P("dp", "seq", None, "mp"),
        ),
        out_specs=(
            P("dp", "seq", None, "mp"),
            P("dp", "seq", None, "mp"),
            P("dp", "seq", "mp", None),
            P("dp", "seq", "mp", None),
            P("dp", "seq", None, "mp"),
            P(None, "mp"),
            P(None, "mp"),
            P(None, "mp"),
        ),
        check_vma=False,
    )
```

profile of v0, /device:TPU:1, one launch (start us, length us, event | category | flops | bytes accessed | tf_op | source)
XLA Modules:
  0.0 293.3 jit_solution(2683088876785404808)
XLA Ops:
  22.1 10.3 %all-gather = f32[4,1,8,2]{2,3,1,0:T(2,128)S(1)} all-gather(f32[1,1,8,2]{2,3,1,0:T(2,128)S(1)} %copy.530), channel_id=2, replica_groups=mesh['seq'=4,'dp'=2,'mp'=4] {'seq'}, dimensions={0}, use_global_device_ids=true | all-gather | bytes 320 | tf_op jit(solution)/shard_map/all_gather | solution.py:94
  32.8 2.2 copy.538
  36.1 29.0 %all-gather.8.cloned.1.call-done = f32[32,2,64,128]{3,2,1,0:T(8,128)} async-done(((f32[8,2,64,128]{3,2,1,0:T(8,128)}), f32[32,2,64,128]{3,2,1,0:T(8,128)}) %all-gather.8.cloned.1.call-update) | async-done | bytes 2097168 | tf_op jit(solution)/shard_map/all_gather | solution.py:16
  65.1 5.2 %while.63 = (s32[]{:T(128)}, f32[1,8,2,64,128]{4,3,2,1,0:T(8,128)S(1)}, s32[]{:T(128)}, f32[4,1,8,2,64,128]{5,4,3,2,1,0:T(8,128)}, f32[4,1,8,2]{2,3,1,0:T(2,128)...) while((s32[]{:T(128)}, f32[1,8,2,64,128]{4,3,2,1,0:T(8,128)S(1)}, s32[]{:T(128)}, ...), condition=%wide.region_10.11_spmd.clone, body=%wide.region_9.10_spmd.clone.sunk | while | flops 524296 | bytes 1573359 | solution.py:29
  70.3 41.7 %all-gather.6.cloned.1.call-done = f32[32,2,64,128]{3,2,1,0:T(8,128)} async-done(((f32[8,2,64,128]{3,2,1,0:T(8,128)}), f32[32,2,64,128]{3,2,1,0:T(8,128)}) %all-gather.6.cloned.1.call-update) | async-done | bytes 2097168 | tf_op jit(solution)/shard_map/all_gather | solution.py:103
  113.8 2.6 fusion.126
  117.3 39.9 %while.62 = (s32[]{:T(128)}, f32[1,8,2,64,128]{4,3,2,1,0:T(8,128)S(1)}, bf16[2,1,128,8,2,64]{2,5,4,3,1,0:T(8,128)(2,1)}, f32[2,1,8,2,64,128]{5,4,3,2,1,0:T(8,128...) while((s32[]{:T(128)}, ...), condition=%wide.region_8.9_spmd.clone, body=%wide.region_5.8_spmd.clone.sunk | while | flops 405264384 | bytes 27010904 | solution.py:154
  120.7 2.2 exponential_select_fusion.5
  130.5 2.1 copy.675
  132.6 3.6 %fusion.214 = bf16[2,1,128,8,2,64]{2,5,4,3,1,0:T(8,128)(2,1)} fusion(bf16[2,1,128,8,2,64]{2,5,4,3,1,0:T(8,128)(2,1)} %get-tuple-element.1556, s32[]{:T(128)S(6)} %copy.711, f32[1,128,8,2,64]{1,4,3,2,0:T(8,128)} %fusion.213, f32[128,8,2]{0,2,1:T(2,128)S(1)} %copy.673, f32[128,8,2]{0,2,1:T(2,128)S(1)} %copy.674, f32[128,128,8]{1,0,2:T(8,128)} %copy.675, ...), kind=kOutput, calls=%fused_computation.10.clone.1 | convolution fusion | flops 102367232 | bytes 2667520 | tf_op jit(solution)/shard_map/jvp()/while/body/eval_jaxpr/rtsgh,rsghp->rtghp/dot_general | solution.py:53
  140.6 2.2 exponential_select_fusion.5
  150.5 2.1 copy.675
  152.5 3.6 %fusion.214 = bf16[2,1,128,8,2,64]{2,5,4,3,1,0:T(8,128)(2,1)} fusion(bf16[2,1,128,8,2,64]{2,5,4,3,1,0:T(8,128)(2,1)} %get-tuple-element.1556, s32[]{:T(128)S(6)} %copy.711, f32[1,128,8,2,64]{1,4,3,2,0:T(8,128)} %fusion.213, f32[128,8,2]{0,2,1:T(2,128)S(1)} %copy.673, f32[128,8,2]{0,2,1:T(2,128)S(1)} %copy.674, f32[128,128,8]{1,0,2:T(8,128)} %copy.675, ...), kind=kOutput, calls=%fused_computation.10.clone.1 | convolution fusion | flops 102367232 | bytes 2667520 | tf_op jit(solution)/shard_map/jvp()/while/body/eval_jaxpr/rtsgh,rsghp->rtghp/dot_general | solution.py:53
  161.0 72.8 %while.64 = (s32[]{:T(128)}, f32[8,2]{1,0:T(8,128)}, f32[8,2]{0,1:T(2,128)}, f32[8,2]{1,0:T(8,128)S(1)}, f32[1,8,2,64,128]{4,3,2,1,0:T(8,128)S(1)}, /*index=5*/b...) while((s32[]{:T(128)}, f32[8,2]{1,0:T(8,128)}, ...), condition=%wide.region_24.25_spmd.clone, body=%wide.region_11.24_spmd.clone.sunk | while | flops 1015154816 | bytes 64191552 | solution.py:154
  161.8 1.9 constant_dynamic-slice_fusion.4
  181.6 2.3 fusion.241
  186.6 1.9 fusion.244
  191.4 2.8 fusion.247
  198.2 1.9 constant_dynamic-slice_fusion.4
  218.0 2.3 fusion.241
  223.0 1.9 fusion.244
  227.8 2.8 fusion.247
  234.6 16.4 %all-reduce.2 = (f32[8,2]{0,1:T(2,128)}, f32[8,2]{0,1:T(2,128)}, f32[8,2]{0,1:T(2,128)}) all-reduce(f32[8,2]{0,1:T(2,128)S(1)} %copy-done.34, f32[8,2]{0,1:T(2,128)S(1)} %copy.556, f32[8,2]{0,1:T(2,128)S(1)} %copy.557), channel_id=1, replica_groups=mesh['seq'=4,'dp'=2,'mp'=4] {'seq','dp'}, use_global_device_ids=true, to_apply=%region_27.28 | all-reduce | flops 48 | bytes 384 | tf_op jit(solution)/shard_map/psum | solution.py:200
  259.3 25.7 %reduce-scatter.3.cloned.1.call-done = f32[1,256,2,128]{3,1,0,2:T(8,128)} async-done(((f32[1,256,8,128]{3,1,0,2:T(8,128)}), f32[1,256,2,128]{3,1,0,2:T(8,128)}) %reduce-scatter.3.cloned.1.call-update) | async-done | bytes 262160 | tf_op jit(solution)/shard_map/reduce_scatter | solution.py:197
  (356 shorter events, 115.6 us)
Async XLA Ops:
  7.2 8.5 %copy-start.14 = (bf16[1,256,8,128]{3,2,1,0:T(8,128)(2,1)S(1)}, bf16[1,256,8,128]{3,2,1,0:T(8,128)(2,1)}, u32[]{:S(2)}) copy-start(bf16[1,256,8,128]{3,2,1,0:T(8,128)(2,1)} %param.17) | copy-start | bytes 1572868
  7.2 57.9 %all-gather.8.cloned.1.call-start = ((), (), s32[]{:S(2)}) async-start(), calls=%async_computation.5 | async-start | bytes 2621440 | tf_op jit(solution)/shard_map/all_gather | solution.py:16
  16.9 95.0 %all-gather.6.cloned.1.call-start = ((), (), s32[]{:S(2)}) async-start(), calls=%async_computation.4 | async-start | bytes 2621440 | tf_op jit(solution)/shard_map/all_gather | solution.py:103
  19.2 238.3 %reduce-scatter.5.cloned.1.call-start = ((), (), s32[]{:S(2)}) async-start(), calls=%async_computation.3 | async-start | bytes 1310720 | tf_op jit(solution)/shard_map/reduce_scatter | solution.py:198
  161.0 3.9 %copy-start.1 = (f32[2,1,128,8,128]{4,2,3,1,0:T(8,128)}, f32[2,1,128,8,128]{4,2,3,1,0:T(8,128)S(1)}, u32[]{:S(2)}) copy-start(f32[2,1,128,8,128]{4,2,3,1,0:T(8,128)S(1)} %get-tuple-element.1663) | copy-start | bytes 3145732 | tf_op jit(solution)/shard_map/transpose(jvp())/while
  161.0 3.9 %copy-start.9 = (f32[2,1,8,2,64,128]{5,4,3,2,1,0:T(8,128)S(1)}, f32[2,1,8,2,64,128]{5,4,3,2,1,0:T(8,128)}, u32[]{:S(2)}) copy-start(f32[2,1,8,2,64,128]{5,4,3,2,1,0:T(8,128)} %get-tuple-element.1660) | copy-start | bytes 3145732 | tf_op jit(solution)/shard_map/transpose(jvp())/while
  161.0 4.0 %copy-start.4 = (f32[2,1,128,8,128]{4,2,3,1,0:T(8,128)S(1)}, f32[2,1,128,8,128]{4,2,3,1,0:T(8,128)}, u32[]{:S(2)}) copy-start(f32[2,1,128,8,128]{4,2,3,1,0:T(8,128)} %get-tuple-element.1662) | copy-start | bytes 3145732 | tf_op jit(solution)/shard_map/transpose(jvp())/while
  167.9 8.7 %copy-start.29 = (pred[128]{0:T(512)(128)(4,1)}, pred[128]{0:T(512)(128)(4,1)S(1)}, u32[]{:S(2)}) copy-start(pred[128]{0:T(512)(128)(4,1)S(1)} %broadcast_compare_fusion.5) | copy-start | bytes 388 | tf_op jit(solution)/shard_map/transpose(jvp())/while
  183.9 6.7 %copy-start.32 = (f32[8,2]{0,1:T(2,128)S(1)}, f32[8,2]{0,1:T(2,128)}, u32[]{:S(2)}) copy-start(f32[8,2]{0,1:T(2,128)} %get-tuple-element.1632) | copy-start | bytes 196 | tf_op jit(solution)/shard_map/transpose(jvp())/while
  183.9 7.5 %copy-start.20 = (f32[8,2]{1,0:T(8,128)S(1)}, f32[8,2]{1,0:T(8,128)}, u32[]{:S(2)}) copy-start(f32[8,2]{1,0:T(8,128)} %get-tuple-element.1631) | copy-start | bytes 196 | tf_op jit(solution)/shard_map/transpose(jvp())/while
  183.9 7.5 %copy-start.35 = (f32[8,2]{1,0:T(8,128)S(1)}, f32[8,2]{1,0:T(8,128)}, u32[]{:S(2)}) copy-start(f32[8,2]{1,0:T(8,128)} %get-tuple-element.1536) | copy-start | bytes 196 | tf_op jit(solution)/shard_map/transpose(jvp())/while
  186.6 7.6 %copy-start.26 = (f32[2,1,128,8,2]{2,0,4,3,1:T(2,128)S(1)}, f32[2,1,128,8,2]{2,0,4,3,1:T(2,128)}, u32[]{:S(2)}) copy-start(f32[2,1,128,8,2]{2,0,4,3,1:T(2,128)} %get-tuple-element.1638) | copy-start | bytes 49156 | tf_op jit(solution)/shard_map/transpose(jvp())/while
  197.4 3.9 %copy-start.1 = (f32[2,1,128,8,128]{4,2,3,1,0:T(8,128)}, f32[2,1,128,8,128]{4,2,3,1,0:T(8,128)S(1)}, u32[]{:S(2)}) copy-start(f32[2,1,128,8,128]{4,2,3,1,0:T(8,128)S(1)} %get-tuple-element.1663) | copy-start | bytes 3145732 | tf_op jit(solution)/shard_map/transpose(jvp())/while
  197.4 3.9 %copy-start.9 = (f32[2,1,8,2,64,128]{5,4,3,2,1,0:T(8,128)S(1)}, f32[2,1,8,2,64,128]{5,4,3,2,1,0:T(8,128)}, u32[]{:S(2)}) copy-start(f32[2,1,8,2,64,128]{5,4,3,2,1,0:T(8,128)} %get-tuple-element.1660) | copy-start | bytes 3145732 | tf_op jit(solution)/shard_map/transpose(jvp())/while
  197.4 4.0 %copy-start.4 = (f32[2,1,128,8,128]{4,2,3,1,0:T(8,128)S(1)}, f32[2,1,128,8,128]{4,2,3,1,0:T(8,128)}, u32[]{:S(2)}) copy-start(f32[2,1,128,8,128]{4,2,3,1,0:T(8,128)} %get-tuple-element.1662) | copy-start | bytes 3145732 | tf_op jit(solution)/shard_map/transpose(jvp())/while
  204.3 8.7 %copy-start.29 = (pred[128]{0:T(512)(128)(4,1)}, pred[128]{0:T(512)(128)(4,1)S(1)}, u32[]{:S(2)}) copy-start(pred[128]{0:T(512)(128)(4,1)S(1)} %broadcast_compare_fusion.5) | copy-start | bytes 388 | tf_op jit(solution)/shard_map/transpose(jvp())/while
  220.3 6.7 %copy-start.32 = (f32[8,2]{0,1:T(2,128)S(1)}, f32[8,2]{0,1:T(2,128)}, u32[]{:S(2)}) copy-start(f32[8,2]{0,1:T(2,128)} %get-tuple-element.1632) | copy-start | bytes 196 | tf_op jit(solution)/shard_map/transpose(jvp())/while
  220.3 7.5 %copy-start.20 = (f32[8,2]{1,0:T(8,128)S(1)}, f32[8,2]{1,0:T(8,128)}, u32[]{:S(2)}) copy-start(f32[8,2]{1,0:T(8,128)} %get-tuple-element.1631) | copy-start | bytes 196 | tf_op jit(solution)/shard_map/transpose(jvp())/while
  220.3 7.5 %copy-start.35 = (f32[8,2]{1,0:T(8,128)S(1)}, f32[8,2]{1,0:T(8,128)}, u32[]{:S(2)}) copy-start(f32[8,2]{1,0:T(8,128)} %get-tuple-element.1536) | copy-start | bytes 196 | tf_op jit(solution)/shard_map/transpose(jvp())/while
  223.0 7.6 %copy-start.26 = (f32[2,1,128,8,2]{2,0,4,3,1:T(2,128)S(1)}, f32[2,1,128,8,2]{2,0,4,3,1:T(2,128)}, u32[]{:S(2)}) copy-start(f32[2,1,128,8,2]{2,0,4,3,1:T(2,128)} %get-tuple-element.1638) | copy-start | bytes 49156 | tf_op jit(solution)/shard_map/transpose(jvp())/while
  233.8 17.2 %copy-start.28 = (f32[2,1,128,8,2]{2,0,4,3,1:T(2,128)S(1)}, f32[2,1,128,8,2]{2,0,4,3,1:T(2,128)}, u32[]{:S(2)}) copy-start(f32[2,1,128,8,2]{2,0,4,3,1:T(2,128)} %get-tuple-element.1701) | copy-start | bytes 49156
  233.8 17.8 %copy-start.13 = (bf16[2,1,128,8,2,64]{2,5,4,3,1,0:T(8,128)(2,1)S(1)}, bf16[2,1,128,8,2,64]{2,5,4,3,1,0:T(8,128)(2,1)}, u32[]{:S(2)}) copy-start(bf16[2,1,128,8,2,64]{2,5,4,3,1,0:T(8,128)(2,1)} %get-tuple-element.678) | copy-start | bytes 1572868
  233.8 51.2 %reduce-scatter.3.cloned.1.call-start = ((), (), s32[]{:S(2)}) async-start(), calls=%async_computation.2 | async-start | bytes 1310720 | tf_op jit(solution)/shard_map/reduce_scatter | solution.py:197
  233.8 20.0 %copy-start.12 = (bf16[2,1,128,8,2,64]{2,5,4,3,1,0:T(8,128)(2,1)S(1)}, bf16[2,1,128,8,2,64]{2,5,4,3,1,0:T(8,128)(2,1)}, u32[]{:S(2)}) copy-start(bf16[2,1,128,8,2,64]{2,5,4,3,1,0:T(8,128)(2,1)} %get-tuple-element.1698) | copy-start | bytes 1572868
  (40 other events, 83.3 us)
Sparse Core Ops, SparseCore 0:
  17.1 48.0 all-gather.7
  67.3 44.6 all-gather.5
  233.9 23.5 reduce-scatter.4
  260.1 24.8 reduce-scatter.2
where the time goes:
time: 296 us; the launch traced here: 293 us
  waiting for transfers between devices  98.4 us (33%)
  local copies, waits for them, and re-layouts  71.3 us (24%)
  other arithmetic  40.5 us (14%)
  matrix products  39.9 us (13%)
  blocking collectives  26.6 us (9%)
  between operations  15.3 us (5%)
    all_gather x1, waiting for transfers between devices, fold_states(): shard_piece = lax.all_gather(summary_state, 'seq', axis=0, tiled=True)  41.7 us
    all_gather x1, waiting for transfers between devices, prefix(): everything = jax.tree.map(lambda part: lax.all_gather(part, axis), shard)  29 us
    reduce_scatter x1, waiting for transfers between devices, local(): lax.psum_scatter(keys_grad, 'mp', scatter_dimension=2, tiled=True)  25.7 us
    psum x1, blocking collectives, local(): lax.psum((rate_grad, bias_grad, gain_grad), ('seq', 'dp'))  16.4 us
    dot_general x6, matrix products, block_forward(): jnp.einsum('rtsgh,rsghp->rtghp', mixing, head_vals, precision=triple)  14.7 us
    unnamed x37, local copies, waits for them, and re-layouts  12.1 us
    another operation x6, other arithmetic, decay_terms(): cumulative = jnp.cumsum(log_decay, axis=1)  10.6 us
    all_gather x1, blocking collectives, fold_states(): all_carried = lax.all_gather(passed_forward, 'seq', axis=0, tiled=True)  10.3 us
  transfers between devices with their start and end apart: 4, of which 4 were waited for; matrix products, arithmetic and copies ran while one was open for 7% of the time, Pallas kernels for 0%

commit v1 on v0

v1 whole, which is shorter than its diff:
```python
import functools

import jax
import jax.numpy as jnp
from jax import lax
from jax.experimental import pallas as pl
from jax.experimental.pallas import tpu as pltpu
from jax.sharding import PartitionSpec as P

P_SIZE = 64
F32 = jnp.float32
BF16 = jnp.bfloat16
MESH = pl.DeviceIdType.MESH
NN = ((1,), (0,))
NT = ((1,), (1,))


def mm(a, b, dims=NN):
    return lax.dot_general(a, b, (dims, ((), ())), preferred_element_type=F32)


def split2(a):
    hi = a.astype(BF16)
    return hi, (a - hi.astype(F32)).astype(BF16)


def split3(a):
    hi = a.astype(BF16)
    rest = a - hi.astype(F32)
    mid = rest.astype(BF16)
    return hi, mid, (rest - mid.astype(F32)).astype(BF16)


def left2(a, b, dims=NN):
    hi, lo = split2(a)
    return mm(hi, b, dims) + mm(lo, b, dims)


def right2(a, b, dims=NN):
    hi, lo = split2(b)
    return mm(a, hi, dims) + mm(a, lo, dims)


def left3(a, b, dims=NN):
    hi, mid, lo = split3(a)
    return mm(hi, b, dims) + mm(mid, b, dims) + mm(lo, b, dims)


def right3(a, b, dims=NN):
    hi, mid, lo = split3(b)
    return mm(a, hi, dims) + mm(a, mid, dims) + mm(a, lo, dims)


def both2(a, b, dims=NN):
    ah, al = split2(a)
    bh, bl = split2(b)
    return mm(ah, bh, dims) + mm(al, bh, dims) + mm(ah, bl, dims)


def kernel(
    nseq, ndp, nmp, L, G, H, N,
    x_ref, b_ref, c_ref, dy_ref, raw_ref, doc_ref, par_ref, skip_ref,
    y_out, dx_out, db_out, dc_out, step_out, small_out,
    wide, xg, bg, cg, gg, bt, ct, gt, tab, mask, prow,
    loc_f, loc_b, s_in, s_out, d_out, d_in,
    ybuf, dxbuf, part, rows_r, rows_k, zrow, skiprow,
    rbuf, sbuf,
    f_send, f_recv, b_send, b_recv, m_send, m_recv, p_send, p_recv,
):
    hp = H * P_SIZE
    gl = G // nmp
    npar = nseq * ndp
    gh = G * H
    me_s, me_d, me_m = lax.axis_index("seq"), lax.axis_index("dp"), lax.axis_index("mp")
    me_p = me_s * ndp + me_d
    last = nseq - 1

    barrier = pltpu.get_barrier_semaphore()

    @pl.loop(1, nmp)
    def _(j):
        pl.semaphore_signal(
            barrier, inc=1, device_id={"mp": lax.rem(me_m + j, nmp)}, device_id_type=MESH
        )

    @pl.loop(1, npar)
    def _(j):
        to = lax.rem(me_p + j, npar)
        pl.semaphore_signal(
            barrier,
            inc=1,
            device_id={"seq": to // ndp, "dp": lax.rem(to, ndp)},
            device_id_type=MESH,
        )

    for src, dst in ((x_ref, xg), (b_ref, bg), (c_ref, cg), (dy_ref, gg)):
        width = src.shape[1]
        wide[:, :width] = src[...].astype(F32)
        for g in range(G):
            block = wide[pl.ds(g, L, stride=G), :width]
            dst[g] = block.astype(BF16)
            if dst is bg:
                bt[g] = block.T.astype(BF16)
            if dst is cg:
                ct[g] = block.T.astype(BF16)
            if dst is gg:
                gt[g] = block.T.astype(BF16)

    i0 = lax.broadcasted_iota(jnp.int32, (L, L), 0)
    i1 = lax.broadcasted_iota(jnp.int32, (L, L), 1)
    upper = jnp.where(i0 <= i1, 1.0, 0.0).astype(BF16)
    raw = raw_ref[...]
    log_rate, bias = par_ref[:, 0:1], par_ref[:, 1:2]
    z = raw + bias
    dt = jnp.maximum(z, 0.0) + jnp.log1p(jnp.exp(-jnp.abs(z)))
    rate = jnp.exp(log_rate)
    cum = left3(-dt * rate, upper)
    docs = mm(jnp.broadcast_to(doc_ref[...].astype(F32), (8, L)).astype(BF16), upper)
    doc_row = docs[0:1]
    entry = jnp.where(doc_row == 0.0, jnp.exp(cum), 0.0)
    tail = doc_row == doc_row[:, L - 1 : L]
    weight = jnp.where(tail, jnp.exp(cum[:, L - 1 : L] - cum), 0.0) * dt
    doc_col = docs.T[:, 0:1]
    mask[...] = jnp.where((i0 >= i1) & (doc_col == doc_row), 0.0, -1e30)
    lane_head = lax.broadcasted_iota(jnp.int32, (1, hp), 1) // P_SIZE
    for g in range(G):
        for q, val in enumerate((cum, dt, weight, entry)):
            tab[g, q * H : (q + 1) * H, :] = val[g * H : (g + 1) * H]
        passed = entry[g * H : g * H + 1, L - 1 : L]
        passed = jnp.broadcast_to(passed, (1, hp))
        for h in range(1, H):
            passed = jnp.where(
                lane_head == h, entry[g * H + h : g * H + h + 1, L - 1 : L], passed
            )
        prow[g] = passed

    lanes_l = lax.broadcasted_iota(jnp.int32, (L, hp), 1) // P_SIZE

    def spread(cols, first):
        val = jnp.broadcast_to(cols[:, first : first + 1], (L, hp))
        for h in range(1, H):
            val = jnp.where(lanes_l == h, cols[:, first + h : first + h + 1], val)
        return val

    def send_f(g):
        return pltpu.make_async_remote_copy(
            src_ref=s_out.at[g], dst_ref=s_in.at[g],
            send_sem=f_send.at[g], recv_sem=f_recv.at[g],
            device_id={"seq": jnp.minimum(me_s + 1, last)}, device_id_type=MESH,
        )

    def send_b(g):
        return pltpu.make_async_remote_copy(
            src_ref=d_in.at[g], dst_ref=d_out.at[g],
            send_sem=b_send.at[g], recv_sem=b_recv.at[g],
            device_id={"seq": jnp.maximum(me_s - 1, 0)}, device_id_type=MESH,
        )

    def send_m(g, j):
        return pltpu.make_async_remote_copy(
            src_ref=part.at[g], dst_ref=rbuf.at[lax.rem(g, gl), j],
            send_sem=m_send.at[g], recv_sem=m_recv.at[lax.rem(g, gl), j],
            device_id={"mp": g // gl}, device_id_type=MESH,
        )

    pl.semaphore_wait(barrier, (nmp - 1) + (npar - 1))

    @pl.loop(0, G)
    def _(g):
        cols = tab[g].T
        loc_f[g] = right2(bt[g], xg[g].astype(F32) * spread(cols, 2 * H))
        loc_b[g] = right2(ct[g], gg[g].astype(F32) * spread(cols, 3 * H))

        @pl.when(me_s == 0)
        def _():
            s_in[g] = jnp.zeros((N, hp), F32)
            s_out[g] = loc_f[g]
            if nseq > 1:
                send_f(g).start()

        @pl.when(me_s == last)
        def _():
            d_out[g] = jnp.zeros((N, hp), F32)
            d_in[g] = loc_b[g]
            if nseq > 1:
                send_b(g).start()

    def local(g):
        cols = tab[g].T
        trow = tab[g]
        xb, bb, cb, gb = xg[g], bg[g], cg[g], gg[g]
        scores = mm(cb, bt[g])
        grad_s = None
        y = None
        dxt = []
        pr = jnp.zeros((8, L), F32)
        head_row = lax.broadcasted_iota(jnp.int32, (8, 128), 0)
        for h in range(H):
            xm = jnp.where(lanes_l == h, xb.astype(F32), 0.0).astype(BF16)
            dm = mm(gb, xm, NT)
            decay = jnp.exp(cols[:, h : h + 1] - trow[h : h + 1] + mask[...])
            w = decay * trow[H + h : H + h + 1]
            mix = scores * w
            dmw = dm * w
            grad_s = dmw if grad_s is None else grad_s + dmw
            q = dmw * scores
            rows_k[g, h : h + 1, :] = jnp.sum(q, axis=0, keepdims=True)
            folded = q[:, 0:128]
            for j in range(128, L, 128):
                folded = folded + q[:, j : j + 128]
            pick = jnp.where(head_row == h, 1.0, 0.0).astype(BF16)
            pr = pr + right3(pick, folded, NT)
            hi, lo = split2(mix)
            now = mm(hi, xm) + mm(lo, xm)
            y = now if y is None else y + now
            gth = gt[g, h * P_SIZE : (h + 1) * P_SIZE, :]
            dxt.append(mm(gth, hi) + mm(gth, lo))
        rows_r[g] = pr
        ybuf[g] = y
        dxbuf[g] = (dxt[0] if H == 1 else jnp.concatenate(dxt, axis=0)).T
        hi, lo = split2(grad_s)
        part[g, 1] = mm(hi, bb) + mm(lo, bb)
        part[g, 0] = (mm(ct[g], hi) + mm(ct[g], lo)).T

    head8 = lax.broadcasted_iota(jnp.int32, (8, hp), 0)
    sel = jnp.where(head8 == lax.broadcasted_iota(jnp.int32, (8, hp), 1) // P_SIZE, 1.0, 0.0)
    sel = sel.astype(BF16)

    def finish(g):
        cols = tab[g].T
        wl, el = spread(cols, 2 * H), spread(cols, 3 * H)
        xb, bb, cb, gb = xg[g], bg[g], cg[g], gg[g]
        xf, gf = xb.astype(F32), gb.astype(F32)
        sin, dso = s_in[g], d_out[g]
        gain = skip_ref[pl.ds(g, 1), :]
        yo = right2(cb, sin) * el
        dxo = right2(bb, dso) * wl
        ybuf[g] = ybuf[g] + yo + gain * xf
        dxbuf[g] = dxbuf[g] + dxo + gain * gf
        e_rows = right3(sel, gf * yo, NT)
        f_rows = right3(sel, xf * dxo, NT)
        rows_r[g] = rows_r[g] + e_rows
        rows_k[g, 0:H, :] = rows_k[g, 0:H, :] + f_rows[0:H]
        part[g, 1] = part[g, 1] + both2(gf * el, sin, NT)
        part[g, 0] = part[g, 0] + both2(xf * wl, dso, NT)
        skiprow[g] = jnp.sum(gf * xf, axis=0, keepdims=True)
        zrow[g] = jnp.sum((prow[g] * sin + loc_f[g]) * dso, axis=0, keepdims=True)

        @pl.when(g // gl != me_m)
        def _():
            send_m(g, me_m).start()

    lag_f = me_s - 1
    lag_b = last - me_s - 1
    lag = jnp.maximum(jnp.maximum(lag_f, lag_b), 0)

    @pl.loop(0, G + max(nseq - 2, 0))
    def _(i):
        @pl.when(i < G)
        def _():
            local(i)

        if nseq > 1:
            gf = i - lag_f
            gb = i - lag_b

            @pl.when((me_s > 0) & (gf >= 0) & (gf < G))
            def _():
                send_f(gf).wait_recv()

                @pl.when(me_s < last)
                def _():
                    s_out[gf] = prow[gf] * s_in[gf] + loc_f[gf]
                    send_f(gf).start()

            @pl.when((me_s < last) & (gb >= 0) & (gb < G))
            def _():
                send_b(gb).wait_recv()

                @pl.when(me_s > 0)
                def _():
                    d_in[gb] = prow[gb] * d_out[gb] + loc_b[gb]
                    send_b(gb).start()

        g = i - lag

        @pl.when((g >= 0) & (g < G))
        def _():
            finish(g)

    k_all = jnp.concatenate([rows_k[g, 0:H, :] for g in range(G)], axis=0)
    r_all = jnp.concatenate([rows_r[g, 0:H, :] for g in range(G)], axis=0)
    zcol = jnp.concatenate(
        [
            jnp.sum(jnp.where(lane_head == h, zrow[g], 0.0), axis=1, keepdims=True)
            for g in range(G)
            for h in range(H)
        ],
        axis=0,
    )
    dld = left3(r_all - k_all, upper, NT) + zcol
    ddt = k_all / dt - rate * dld
    dz = ddt * (1.0 / (1.0 + jnp.exp(-z)))
    step_out[...] = dz
    rate_g = -jnp.sum(dld * dt, axis=1, keepdims=True) * rate
    bias_g = jnp.sum(dz, axis=1, keepdims=True)
    lane = lax.broadcasted_iota(jnp.int32, (gh, 128), 1)
    mine = jnp.where(lane == 0, rate_g, jnp.where(lane == 1, bias_g, 0.0))
    skip_all = jnp.concatenate([skiprow[g] for g in range(G)], axis=0)
    if hp < 128:
        skip_all = jnp.concatenate([skip_all, jnp.zeros((G, 128 - hp), F32)], axis=1)
    sbuf[me_p] = jnp.concatenate([mine, skip_all], axis=0)

    def send_p(j):
        to = lax.rem(me_p + j, npar)
        return pltpu.make_async_remote_copy(
            src_ref=sbuf.at[me_p], dst_ref=sbuf.at[me_p],
            send_sem=p_send.at[j], recv_sem=p_recv.at[me_p],
            device_id={"seq": to // ndp, "dp": lax.rem(to, ndp)}, device_id_type=MESH,
        )

    @pl.loop(1, npar)
    def _(j):
        send_p(j).start()

    for buf, dst in ((ybuf, y_out), (dxbuf, dx_out)):
        for g in range(G):
            wide[pl.ds(g, L, stride=G), :hp] = buf[g]
        dst[...] = wide[:, :hp].astype(BF16)

    for a in range(gl):
        g = me_m * gl + a

        @pl.loop(1, nmp)
        def _(j):
            frm = lax.rem(me_m + j, nmp)
            pltpu.make_async_copy(part.at[g], rbuf.at[a, frm], m_recv.at[a, frm]).wait()
            part[g] = part[g] + rbuf[a, frm]

        db_out[:, a * N : (a + 1) * N] = part[g, 0].astype(BF16)
        dc_out[:, a * N : (a + 1) * N] = part[g, 1].astype(BF16)

    @pl.loop(1, npar)
    def _(j):
        frm = lax.rem(me_p + j, npar)
        pltpu.make_async_copy(sbuf.at[frm], sbuf.at[frm], p_recv.at[frm]).wait()

    total = sbuf[0]
    for j in range(1, npar):
        total = total + sbuf[j]
    small_out[...] = total

    @pl.loop(1, npar)
    def _(j):
        send_p(j).wait_send()

    @pl.loop(0, G)
    def _(g):
        @pl.when(g // gl != me_m)
        def _():
            send_m(g, me_m).wait_send()

        if nseq > 1:

            @pl.when(me_s < last)
            def _():
                send_f(g).wait_send()

            @pl.when(me_s > 0)
            def _():
                send_b(g).wait_send()


def local(
    nseq, ndp, nmp,
    features, key_projection, query_proj, step_raw, doc_starts,
    log_rate, step_bias, skip_gain, out_grad,
):
    rows, L, G, hp = features.shape
    assert rows == 1
    N = key_projection.shape[-1]
    H = hp // P_SIZE
    gl = G // nmp
    gh = G * H
    npar = nseq * ndp
    raw = jnp.transpose(step_raw[0], (1, 2, 0)).reshape(gh, L)
    par = jnp.stack([log_rate.reshape(gh), step_bias.reshape(gh)], axis=-1)
    gain = jnp.repeat(skip_gain, P_SIZE, axis=1)
    vm = pltpu.VMEM
    nr = -(-4 * H // 8) * 8
    dma = pltpu.SemaphoreType.DMA
    scratch = [
        vm((L * G, max(hp, N)), F32),
        vm((G, L, hp), BF16), vm((G, L, N), BF16), vm((G, L, N), BF16), vm((G, L, hp), BF16),
        vm((G, N, L), BF16), vm((G, N, L), BF16), vm((G, hp, L), BF16),
        vm((G, nr, L), F32), vm((L, L), F32), vm((G, 1, hp), F32),
        vm((G, N, hp), F32), vm((G, N, hp), F32),
        vm((G, N, hp), F32), vm((G, N, hp), F32), vm((G, N, hp), F32), vm((G, N, hp), F32),
        vm((G, L, hp), F32), vm((G, L, hp), F32), vm((G, 2, L, N), F32),
        vm((G, 8, L), F32), vm((G, 8, L), F32), vm((G, 1, hp), F32), vm((G, 1, hp), F32),
        vm((gl, nmp, 2, L, N), F32), vm((npar, gh + G, 128), F32),
        dma((G,)), dma((G,)), dma((G,)), dma((G,)), dma((G,)), dma((gl, nmp)),
        dma((npar,)), dma((npar,)),
    ]
    y, dx, db, dc, step, small = pl.pallas_call(
        functools.partial(kernel, nseq, ndp, nmp, L, G, H, N),
        out_shape=(
            jax.ShapeDtypeStruct((L * G, hp), BF16),
            jax.ShapeDtypeStruct((L * G, hp), BF16),
            jax.ShapeDtypeStruct((L, gl * N), BF16),
            jax.ShapeDtypeStruct((L, gl * N), BF16),
            jax.ShapeDtypeStruct((gh, L), F32),
            jax.ShapeDtypeStruct((gh + G, 128), F32),
        ),
        in_specs=[pl.BlockSpec(memory_space=pltpu.VMEM)] * 8,
        out_specs=[pl.BlockSpec(memory_space=pltpu.VMEM)] * 6,
        scratch_shapes=scratch,
        compiler_params=pltpu.CompilerParams(
            collective_id=0, has_side_effects=True, vmem_limit_bytes=56 * 2**20
        ),
    )(
        features.reshape(L * G, hp),
        key_projection.reshape(L * G, N),
        query_proj.reshape(L * G, N),
        out_grad.reshape(L * G, hp),
        raw, doc_starts, par, gain,
    )
    return (
        y.reshape(1, L, G, hp),
        dx.reshape(1, L, G, hp),
        db.reshape(1, L, gl, N),
        dc.reshape(1, L, gl, N),
        jnp.transpose(step.reshape(G, H, L), (2, 0, 1))[None],
        small[:gh, 0].reshape(G, H),
        small[:gh, 1].reshape(G, H),
        small[gh:, :hp].reshape(G, H, P_SIZE).sum(-1),
    )


def solution(mesh):
    sizes = dict(mesh.shape)
    return jax.shard_map(
        functools.partial(local, sizes["seq"], sizes["dp"], sizes["mp"]),
        mesh=mesh,
        in_specs=(
            P("dp", "seq", None, "mp"),
            P("dp", "seq", None, None),
            P("dp", "seq", None, None),
            P("dp", "seq", None, "mp"),
            P("dp", "seq"),
            P(None, "mp"),
            P(None, "mp"),
            P(None, "mp"),
            P("dp", "seq", None, "mp"),
        ),
        out_specs=(
            P("dp", "seq", None, "mp"),
            P("dp", "seq", None, "mp"),
            P("dp", "seq", "mp", None),
            P("dp", "seq", "mp", None),
            P("dp", "seq", None, "mp"),
            P(None, "mp"),
            P(None, "mp"),
            P(None, "mp"),
        ),
        check_vma=False,
    )
```

time: 296 us -> 68.6 us (0.23)
  the two profiles are of different devices: /device:TPU:1 before, /device:TPU:0 now
where the time goes in v1:
time: 68.6 us; the launch traced here: 68.2 us
  Pallas kernels  53.9 us (79%)
  local copies, waits for them, and re-layouts  13.5 us (20%)
    pallas_call x1, Pallas kernels, local(): pl.pallas_call(functools.partial(kernel, nseq, ndp, nmp, L, G, H, N), out...  53.9 us
    unnamed x18, local copies, waits for them, and re-layouts  5.63 us
    reshape x1, local copies, waits for them, and re-layouts, local(): dc.reshape(1, L, gl, N)  1.61 us
    reshape x1, local copies, waits for them, and re-layouts, local(): db.reshape(1, L, gl, N)  1.59 us

profile of v1, /device:TPU:0, one launch (start us, length us, event | category | flops | bytes accessed | tf_op | source)
XLA Modules:
  0.0 68.2 jit_solution(804049752381338247)
XLA Ops:
  0.6 0.8 %copy.31 = f32[8,2]{1,0:T(8,128)S(1)} copy(f32[8,2]{0,1:T(2,128)} %param.14) | data formatting | bytes 128 | tf_op args[5]
  1.4 0.1 stack_reshape.6
  1.5 0.8 %copy.32 = f32[8,2]{1,0:T(8,128)S(1)} copy(f32[8,2]{0,1:T(2,128)} %param.15) | data formatting | bytes 128 | tf_op args[6]
  2.2 0.1 stack_reshape.7
  2.3 0.7 %copy.34.par_ref = f32[16,2]{1,0:T(8,128)} copy(f32[16,2]{0,1:T(2,128)S(1)} %pad_maximum_fusion) | data formatting | bytes 256 | tf_op jit(solution)/shard_map/stack | solution.py:387
  3.0 0.6 reshape.56.raw_ref
  3.7 0.1 copy.33
  3.9 0.7 reshape.57.skip_ref
  4.5 53.9 %shard_map.152 = (bf16[2048,128]{1,0:T(8,128)(2,1)}, bf16[2048,128]{1,0:T(8,128)(2,1)}, bf16[256,256]{1,0:T(8,128)(2,1)}, bf16[256,256]{1,0:T(8,128)(2,1)}, f32[16,256]{1,0:T(8,128)}, /*index=5*/f32[24,128]{1,0:T(8,128)}) custom-call(bf16[2048,128]{1,0:T(8,128)(2,1)} %bitcast.14, bf16[2048,128]{1,0:T(8,128)(2,1)} %bitcast.15, bf16[2048,128]{1,0:T(8,128)(2,1)} %bitcast.16, ...), custom_call_target="tpu_custom_call" | custom-call | tf_op jit(solution)/shard_map/pallas_call | solution.py:405
  58.5 1.0 %slice_reduce_fusion = (f32[16]{0:T(128)S(1)}, f32[16]{0:T(128)S(1)}) fusion(f32[24,128]{1,0:T(8,128)} %get-tuple-element.19), kind=kLoop, calls=%fused_computation | loop fusion | bytes 256 | tf_op jit(solution)/shard_map/slice | solution.py:435
  59.4 0.1 reshape_squeeze.6
  59.5 0.6 copy.35
  60.1 0.1 reshape_squeeze.7
  60.2 0.6 copy.36
  60.9 0.7 %slice.11 = f32[8,128]{1,0:T(8,128)S(1)} slice(f32[24,128]{1,0:T(8,128)} %get-tuple-element.19), slice={[16:24], [0:128]} | slice | bytes 8192 | tf_op jit(solution)/shard_map/slice | solution.py:436
  61.5 0.1 reshape.63
  61.6 0.1 reduce_sum.9
  61.7 0.6 copy.37
  62.4 1.6 %reshape.60 = bf16[1,256,2,128]{3,2,1,0:T(2,128)(2,1)} reshape(bf16[256,256]{1,0:T(8,128)(2,1)} %get-tuple-element.16) | data formatting | bytes 262144 | tf_op jit(solution)/shard_map/reshape | solution.py:431
  63.9 1.6 %reshape.61 = bf16[1,256,2,128]{3,2,1,0:T(2,128)(2,1)} reshape(bf16[256,256]{1,0:T(8,128)(2,1)} %get-tuple-element.17) | data formatting | bytes 262144 | tf_op jit(solution)/shard_map/reshape | solution.py:432
  65.6 0.6 reshape.62
  66.2 0.8 %copy.40 = bf16[1,256,8,128]{3,2,1,0:T(8,128)(2,1)} copy(bf16[1,256,8,128]{3,2,1,0:T(8,128)(2,1)S(1)} %bitcast.13) | data formatting | bytes 1048576
  67.0 0.4 copy-done
  67.4 0.8 %copy.41 = bf16[1,256,8,128]{3,2,1,0:T(8,128)(2,1)} copy(bf16[1,256,8,128]{3,2,1,0:T(8,128)(2,1)S(1)} %bitcast.12) | data formatting | bytes 1048576
  (11 shorter events, 0.2 us)
Async XLA Ops:
  0.6 2.4 %copy-start.2 = (f32[1,256,8,2]{1,3,2,0:T(2,128)S(1)}, f32[1,256,8,2]{1,3,2,0:T(2,128)}, u32[]{:S(2)}) copy-start(f32[1,256,8,2]{1,3,2,0:T(2,128)} %param.12) | copy-start | bytes 49156
  3.0 0.7 copy-start.4
  58.4 7.7 %copy-start.1 = (bf16[2048,128]{1,0:T(8,128)(2,1)S(1)}, bf16[2048,128]{1,0:T(8,128)(2,1)}, u32[]{:S(2)}) copy-start(bf16[2048,128]{1,0:T(8,128)(2,1)} %get-tuple-element.14) | copy-start | bytes 1572868
  63.9 1.6 %copy-start.3 = (f32[16,256]{1,0:T(8,128)S(1)}, f32[16,256]{1,0:T(8,128)}, u32[]{:S(2)}) copy-start(f32[16,256]{1,0:T(8,128)} %get-tuple-element.18) | copy-start | bytes 49156
  66.2 1.2 %copy-start = (bf16[2048,128]{1,0:T(8,128)(2,1)S(1)}, bf16[2048,128]{1,0:T(8,128)(2,1)}, u32[]{:S(2)}) copy-start(bf16[2048,128]{1,0:T(8,128)(2,1)} %get-tuple-element.15) | copy-start | bytes 1572868

commit v2 on v1

--- a/solution.py
+++ b/solution.py
@@ -59,13 +59,14 @@
 
 def kernel(
     nseq, ndp, nmp, L, G, H, N,
-    x_ref, b_ref, c_ref, dy_ref, raw_ref, doc_ref, par_ref, skip_ref,
+    x_ref, b_ref, c_ref, dy_ref, raw_ref, doc_ref, rate_ref, bias_ref, skip_ref,
     y_out, dx_out, db_out, dc_out, step_out, small_out,
+    pars, gains,
     wide, xg, bg, cg, gg, bt, ct, gt, tab, mask, prow,
     loc_f, loc_b, s_in, s_out, d_out, d_in,
     ybuf, dxbuf, part, rows_r, rows_k, zrow, skiprow,
-    rbuf, sbuf,
-    f_send, f_recv, b_send, b_recv, m_send, m_recv, p_send, p_recv,
+    xbuf, rbuf, sbuf,
+    f_send, f_recv, b_send, b_recv, x_send, x_recv, m_send, m_recv, p_send, p_recv,
 ):
     hp = H * P_SIZE
     gl = G // nmp
@@ -74,6 +75,13 @@
     me_s, me_d, me_m = lax.axis_index("seq"), lax.axis_index("dp"), lax.axis_index("mp")
     me_p = me_s * ndp + me_d
     last = nseq - 1
+    fan = 2 if nmp % 2 == 0 else 1
+    pairs = nmp // fan
+    me_x, me_c = me_m // fan, lax.rem(me_m, fan)
+
+    def at(p):
+        return lax.rem(p + (me_x + 1) * (gl * fan), G)
+
 
     barrier = pltpu.get_barrier_semaphore()
 
@@ -109,8 +117,13 @@
     i0 = lax.broadcasted_iota(jnp.int32, (L, L), 0)
     i1 = lax.broadcasted_iota(jnp.int32, (L, L), 1)
     upper = jnp.where(i0 <= i1, 1.0, 0.0).astype(BF16)
-    raw = raw_ref[...]
-    log_rate, bias = par_ref[:, 0:1], par_ref[:, 1:2]
+    raw = jnp.concatenate([raw_ref[g, h : h + 1, :] for h in range(H) for g in range(G)], axis=0)
+    pars[...] = jnp.zeros_like(pars)
+    for q, ref in enumerate((rate_ref, bias_ref, skip_ref)):
+        pars[q * H : (q + 1) * H, 0:G] = ref[...]
+    turned = pars[...].T
+    log_rate = jnp.concatenate([turned[0:G, h : h + 1] for h in range(H)], axis=0)
+    bias = jnp.concatenate([turned[0:G, H + h : H + h + 1] for h in range(H)], axis=0)
     z = raw + bias
     dt = jnp.maximum(z, 0.0) + jnp.log1p(jnp.exp(-jnp.abs(z)))
     rate = jnp.exp(log_rate)
@@ -125,14 +138,19 @@
     lane_head = lax.broadcasted_iota(jnp.int32, (1, hp), 1) // P_SIZE
     for g in range(G):
         for q, val in enumerate((cum, dt, weight, entry)):
-            tab[g, q * H : (q + 1) * H, :] = val[g * H : (g + 1) * H]
-        passed = entry[g * H : g * H + 1, L - 1 : L]
+            for h in range(H):
+                tab[g, q * H + h : q * H + h + 1, :] = val[h * G + g : h * G + g + 1]
+        passed = entry[g : g + 1, L - 1 : L]
         passed = jnp.broadcast_to(passed, (1, hp))
         for h in range(1, H):
             passed = jnp.where(
-                lane_head == h, entry[g * H + h : g * H + h + 1, L - 1 : L], passed
+                lane_head == h, entry[h * G + g : h * G + g + 1, L - 1 : L], passed
             )
         prow[g] = passed
+    gain = jnp.broadcast_to(turned[0:G, 2 * H : 2 * H + 1], (G, hp))
+    for h in range(1, H):
+        gain = jnp.where(lane_head == h, turned[0:G, 2 * H + h : 2 * H + h + 1], gain)
+    gains[...] = gain
 
     lanes_l = lax.broadcasted_iota(jnp.int32, (L, hp), 1) // P_SIZE
 
@@ -156,17 +174,31 @@
             device_id={"seq": jnp.maximum(me_s - 1, 0)}, device_id_type=MESH,
         )
 
-    def send_m(g, j):
+    def send_x(g):
         return pltpu.make_async_remote_copy(
-            src_ref=part.at[g], dst_ref=rbuf.at[lax.rem(g, gl), j],
-            send_sem=m_send.at[g], recv_sem=m_recv.at[lax.rem(g, gl), j],
+            src_ref=part.at[g], dst_ref=xbuf.at[g],
+            send_sem=x_send.at[g], recv_sem=x_recv.at[g],
+            device_id={"mp": me_x * fan + (fan - 1 - me_c)}, device_id_type=MESH,
+        )
+
+    def send_m(g):
+        return pltpu.make_async_remote_copy(
+            src_ref=part.at[g], dst_ref=rbuf.at[lax.rem(g, gl), me_x],
+            send_sem=m_send.at[g], recv_sem=m_recv.at[lax.rem(g, gl), me_x],
             device_id={"mp": g // gl}, device_id_type=MESH,
         )
 
+    def mine_c(g):
+        return lax.rem(g // gl, fan) == me_c
+
+    def mine_x(g):
+        return g // (gl * fan) == me_x
+
     pl.semaphore_wait(barrier, (nmp - 1) + (npar - 1))
 
     @pl.loop(0, G)
-    def _(g):
+    def _(p):
+        g = at(p)
         cols = tab[g].T
         loc_f[g] = right2(bt[g], xg[g].astype(F32) * spread(cols, 2 * H))
         loc_b[g] = right2(ct[g], gg[g].astype(F32) * spread(cols, 3 * H))
@@ -232,7 +264,7 @@
         xb, bb, cb, gb = xg[g], bg[g], cg[g], gg[g]
         xf, gf = xb.astype(F32), gb.astype(F32)
         sin, dso = s_in[g], d_out[g]
-        gain = skip_ref[pl.ds(g, 1), :]
+        gain = gains[pl.ds(g, 1), :]
         yo = right2(cb, sin) * el
         dxo = right2(bb, dso) * wl
         ybuf[g] = ybuf[g] + yo + gain * xf
@@ -246,26 +278,41 @@
         skiprow[g] = jnp.sum(gf * xf, axis=0, keepdims=True)
         zrow[g] = jnp.sum((prow[g] * sin + loc_f[g]) * dso, axis=0, keepdims=True)
 
-        @pl.when(g // gl != me_m)
+        if fan > 1:
+
+            @pl.when(jnp.logical_not(mine_c(g)))
+            def _():
+                send_x(g).start()
+
+    def across(g):
+        @pl.when(mine_c(g))
         def _():
-            send_m(g, me_m).start()
+            if fan > 1:
+                send_x(g).wait_recv()
+                part[g] = part[g] + xbuf[g]
+            if pairs > 1:
+
+                @pl.when(jnp.logical_not(mine_x(g)))
+                def _():
+                    send_m(g).start()
 
     lag_f = me_s - 1
     lag_b = last - me_s - 1
     lag = jnp.maximum(jnp.maximum(lag_f, lag_b), 0)
 
-    @pl.loop(0, G + max(nseq - 2, 0))
+    @pl.loop(0, G + max(nseq - 2, 0) + 1)
     def _(i):
         @pl.when(i < G)
         def _():
-            local(i)
+            local(at(i))
 
         if nseq > 1:
-            gf = i - lag_f
-            gb = i - lag_b
-
-            @pl.when((me_s > 0) & (gf >= 0) & (gf < G))
-            def _():
+            pf = i - lag_f
+            pb = i - lag_b
+
+            @pl.when((me_s > 0) & (pf >= 0) & (pf < G))
+            def _():
+                gf = at(pf)
                 send_f(gf).wait_recv()
 
                 @pl.when(me_s < last)
@@ -273,8 +320,9 @@
                     s_out[gf] = prow[gf] * s_in[gf] + loc_f[gf]
                     send_f(gf).start()
 
-            @pl.when((me_s < last) & (gb >= 0) & (gb < G))
-            def _():
+            @pl.when((me_s < last) & (pb >= 0) & (pb < G))
+            def _():
+                gb = at(pb)
                 send_b(gb).wait_recv()
 
                 @pl.when(me_s > 0)
@@ -282,34 +330,46 @@
                     d_in[gb] = prow[gb] * d_out[gb] + loc_b[gb]
                     send_b(gb).start()
 
-        g = i - lag
-
-        @pl.when((g >= 0) & (g < G))
+        p = i - lag
+
+        @pl.when((p >= 0) & (p < G))
         def _():
-            finish(g)
-
-    k_all = jnp.concatenate([rows_k[g, 0:H, :] for g in range(G)], axis=0)
-    r_all = jnp.concatenate([rows_r[g, 0:H, :] for g in range(G)], axis=0)
+            finish(at(p))
+
+        @pl.when((p >= 1) & (p <= G))
+        def _():
+            across(at(p - 1))
+
+    k_all = jnp.concatenate([rows_k[g, h : h + 1, :] for h in range(H) for g in range(G)], axis=0)
+    r_all = jnp.concatenate([rows_r[g, h : h + 1, :] for h in range(H) for g in range(G)], axis=0)
     zcol = jnp.concatenate(
         [
             jnp.sum(jnp.where(lane_head == h, zrow[g], 0.0), axis=1, keepdims=True)
+            for h in range(H)
             for g in range(G)
-            for h in range(H)
         ],
         axis=0,
     )
     dld = left3(r_all - k_all, upper, NT) + zcol
     ddt = k_all / dt - rate * dld
     dz = ddt * (1.0 / (1.0 + jnp.exp(-z)))
-    step_out[...] = dz
+    for g in range(G):
+        for h in range(H):
+            step_out[g, h : h + 1, :] = dz[h * G + g : h * G + g + 1]
     rate_g = -jnp.sum(dld * dt, axis=1, keepdims=True) * rate
     bias_g = jnp.sum(dz, axis=1, keepdims=True)
     lane = lax.broadcasted_iota(jnp.int32, (gh, 128), 1)
-    mine = jnp.where(lane == 0, rate_g, jnp.where(lane == 1, bias_g, 0.0))
     skip_all = jnp.concatenate([skiprow[g] for g in range(G)], axis=0)
-    if hp < 128:
-        skip_all = jnp.concatenate([skip_all, jnp.zeros((G, 128 - hp), F32)], axis=1)
-    sbuf[me_p] = jnp.concatenate([mine, skip_all], axis=0)
+    skip_g = jnp.concatenate(
+        [
+            jnp.sum(jnp.where(lane_head == h, skip_all, 0.0), axis=1, keepdims=True)
+            for h in range(H)
+        ],
+        axis=0,
+    )
+    sbuf[me_p] = jnp.where(
+        lane == 0, rate_g, jnp.where(lane == 1, bias_g, jnp.where(lane == 2, skip_g, 0.0))
+    )
 
     def send_p(j):
         to = lax.rem(me_p + j, npar)
@@ -330,15 +390,16 @@
 
     for a in range(gl):
         g = me_m * gl + a
-
-        @pl.loop(1, nmp)
-        def _(j):
-            frm = lax.rem(me_m + j, nmp)
-            pltpu.make_async_copy(part.at[g], rbuf.at[a, frm], m_recv.at[a, frm]).wait()
-            part[g] = part[g] + rbuf[a, frm]
-
-        db_out[:, a * N : (a + 1) * N] = part[g, 0].astype(BF16)
-        dc_out[:, a * N : (a + 1) * N] = part[g, 1].astype(BF16)
+        if pairs > 1:
+
+            @pl.loop(1, pairs)
+            def _(j):
+                frm = lax.rem(me_x + j, pairs)
+                pltpu.make_async_copy(part.at[g], rbuf.at[a, frm], m_recv.at[a, frm]).wait()
+                part[g] = part[g] + rbuf[a, frm]
+
+        db_out[a] = part[g, 0]
+        dc_out[a] = part[g, 1]
 
     @pl.loop(1, npar)
     def _(j):
@@ -348,7 +409,10 @@
     total = sbuf[0]
     for j in range(1, npar):
         total = total + sbuf[j]
-    small_out[...] = total
+    turned = total.T
+    for q in range(3):
+        for h in range(H):
+            small_out[q, h : h + 1, :] = turned[q : q + 1, h * G : (h + 1) * G]
 
     @pl.loop(1, npar)
     def _(j):
@@ -356,9 +420,17 @@
 
     @pl.loop(0, G)
     def _(g):
-        @pl.when(g // gl != me_m)
-        def _():
-            send_m(g, me_m).wait_send()
+        if fan > 1:
+
+            @pl.when(jnp.logical_not(mine_c(g)))
+            def _():
+                send_x(g).wait_send()
+
+        if pairs > 1:
+
+            @pl.when(mine_c(g) & jnp.logical_not(mine_x(g)))
+            def _():
+                send_m(g).wait_send()
 
         if nseq > 1:
 
@@ -369,6 +441,16 @@
             @pl.when(me_s > 0)
             def _():
                 send_b(g).wait_send()
+
+
+def leave(y, dx, db, dc, step, small, y_out, dx_out, db_out, dc_out, step_out, *small_outs):
+    y_out[...] = y[...]
+    dx_out[...] = dx[...]
+    for src, dst in ((db, db_out), (dc, dc_out)):
+        dst[...] = jnp.stack([src[a] for a in range(src.shape[0])], axis=1).astype(BF16)
+    step_out[...] = step[...]
+    for q, dst in enumerate(small_outs):
+        dst[...] = small[q]
 
 
 def local(
@@ -383,13 +465,14 @@
     gl = G // nmp
     gh = G * H
     npar = nseq * ndp
-    raw = jnp.transpose(step_raw[0], (1, 2, 0)).reshape(gh, L)
-    par = jnp.stack([log_rate.reshape(gh), step_bias.reshape(gh)], axis=-1)
-    gain = jnp.repeat(skip_gain, P_SIZE, axis=1)
+    raw = jnp.transpose(step_raw[0], (1, 2, 0))
+    pairs = nmp // (2 if nmp % 2 == 0 else 1)
+    npr = -(-3 * H // 8) * 8
     vm = pltpu.VMEM
     nr = -(-4 * H // 8) * 8
     dma = pltpu.SemaphoreType.DMA
     scratch = [
+        vm((npr, 128), F32), vm((G, hp), F32),
         vm((L * G, max(hp, N)), F32),
         vm((G, L, hp), BF16), vm((G, L, N), BF16), vm((G, L, N), BF16), vm((G, L, hp), BF16),
         vm((G, N, L), BF16), vm((G, N, L), BF16), vm((G, hp, L), BF16),
@@ -398,21 +481,21 @@
         vm((G, N, hp), F32), vm((G, N, hp), F32), vm((G, N, hp), F32), vm((G, N, hp), F32),
         vm((G, L, hp), F32), vm((G, L, hp), F32), vm((G, 2, L, N), F32),
         vm((G, 8, L), F32), vm((G, 8, L), F32), vm((G, 1, hp), F32), vm((G, 1, hp), F32),
-        vm((gl, nmp, 2, L, N), F32), vm((npar, gh + G, 128), F32),
-        dma((G,)), dma((G,)), dma((G,)), dma((G,)), dma((G,)), dma((gl, nmp)),
+        vm((G, 2, L, N), F32), vm((gl, pairs, 2, L, N), F32), vm((npar, gh, 128), F32),
+        dma((G,)), dma((G,)), dma((G,)), dma((G,)), dma((G,)), dma((G,)), dma((G,)), dma((gl, pairs)),
         dma((npar,)), dma((npar,)),
     ]
-    y, dx, db, dc, step, small = pl.pallas_call(
+    made = pl.pallas_call(
         functools.partial(kernel, nseq, ndp, nmp, L, G, H, N),
         out_shape=(
             jax.ShapeDtypeStruct((L * G, hp), BF16),
             jax.ShapeDtypeStruct((L * G, hp), BF16),
-            jax.ShapeDtypeStruct((L, gl * N), BF16),
-            jax.ShapeDtypeStruct((L, gl * N), BF16),
-            jax.ShapeDtypeStruct((gh, L), F32),
-            jax.ShapeDtypeStruct((gh + G, 128), F32),
+            jax.ShapeDtypeStruct((gl, L, N), F32),
+            jax.ShapeDtypeStruct((gl, L, N), F32),
+            jax.ShapeDtypeStruct((G, H, L), F32),
+            jax.ShapeDtypeStruct((3, H, G), F32),
         ),
-        in_specs=[pl.BlockSpec(memory_space=pltpu.VMEM)] * 8,
+        in_specs=[pl.BlockSpec(memory_space=pltpu.VMEM)] * 9,
         out_specs=[pl.BlockSpec(memory_space=pltpu.VMEM)] * 6,
         scratch_shapes=scratch,
         compiler_params=pltpu.CompilerParams(
@@ -423,17 +506,33 @@
         key_projection.reshape(L * G, N),
         query_proj.reshape(L * G, N),
         out_grad.reshape(L * G, hp),
-        raw, doc_starts, par, gain,
+        raw, doc_starts, log_rate.T, step_bias.T, skip_gain.T,
     )
+    y, dx, db, dc, step, rate, bias, gain = pl.pallas_call(
+        leave,
+        out_shape=(
+            jax.ShapeDtypeStruct((L * G, hp), BF16),
+            jax.ShapeDtypeStruct((L * G, hp), BF16),
+            jax.ShapeDtypeStruct((L, gl, N), BF16),
+            jax.ShapeDtypeStruct((L, gl, N), BF16),
+            jax.ShapeDtypeStruct((G, H, L), F32),
+            jax.ShapeDtypeStruct((H, G), F32),
+            jax.ShapeDtypeStruct((H, G), F32),
+            jax.ShapeDtypeStruct((H, G), F32),
+        ),
+        in_specs=[pl.BlockSpec(memory_space=pltpu.VMEM)] * 6,
+        out_specs=[pl.BlockSpec(memory_space=pltpu.VMEM)] * 8,
+        compiler_params=pltpu.CompilerParams(vmem_limit_bytes=32 * 2**20),
+    )(*made)
     return (
         y.reshape(1, L, G, hp),
         dx.reshape(1, L, G, hp),
-        db.reshape(1, L, gl, N),
-        dc.reshape(1, L, gl, N),
-        jnp.transpose(step.reshape(G, H, L), (2, 0, 1))[None],
-        small[:gh, 0].reshape(G, H),
-        small[:gh, 1].reshape(G, H),
-        small[gh:, :hp].reshape(G, H, P_SIZE).sum(-1),
+        db[None],
+        dc[None],
+        jnp.transpose(step, (2, 0, 1))[None],
+        rate.T,
+        bias.T,
+        gain.T,
     )
 
 

time: 68.6 us -> 55 us (0.80)
  the two profiles are of different devices: /device:TPU:0 before, /device:TPU:1 now
where the time goes in v2:
time: 55 us; the launch traced here: 54.6 us
  Pallas kernels  48.6 us (88%)
  local copies, waits for them, and re-layouts  5.37 us (10%)
  between operations  0.66 us (1%)
    pallas_call x1, Pallas kernels, local(): pl.pallas_call(functools.partial(kernel, nseq, ndp, nmp, L, G, H, N), out...  47.2 us
    unnamed x12, local copies, waits for them, and re-layouts  5.37 us
    pallas_call x1, Pallas kernels, local(): pl.pallas_call(leave, out_shape=(jax.ShapeDtypeStruct((L * G, hp), BF16),...  1.42 us

profile of v2, /device:TPU:1, one launch (start us, length us, event | category | flops | bytes accessed | tf_op | source)
XLA Modules:
  0.0 54.6 jit_solution(674198515458879673)
XLA Ops:
  0.6 47.2 %shard_map.152 = (bf16[2048,128]{1,0:T(8,128)(2,1)}, bf16[2048,128]{1,0:T(8,128)(2,1)}, f32[2,256,128]{2,1,0:T(8,128)}, f32[2,256,128]{2,1,0:T(8,128)}, f32[8,2,256]{2,1,0:T(2,128)}, /*index=5*/f32[3,2,8]{2,1,0:T(2,128)}) custom-call(bf16[2048,128]{1,0:T(8,128)(2,1)} %bitcast.20, bf16[2048,128]{1,0:T(8,128)(2,1)} %bitcast.21, bf16[2048,128]{1,0:T(8,128)(2,1)} %bitcast.22, ...), custom_call_target="tpu_custom_call" | custom-call | tf_op jit(solution)/shard_map/pallas_call | solution.py:488
  47.8 0.0 copy-start.5
  47.8 0.7 %copy-done.5 = f32[3,2,8]{2,1,0:T(2,128)S(1)} copy-done((f32[3,2,8]{2,1,0:T(2,128)S(1)}, f32[3,2,8]{2,1,0:T(2,128)}, u32[]{:S(2)}) %copy-start.5) | copy-done | bytes 216
  48.5 0.0 copy-start
  48.5 1.0 %copy-done = bf16[2048,128]{1,0:T(8,128)(2,1)S(1)} copy-done((bf16[2048,128]{1,0:T(8,128)(2,1)S(1)}, bf16[2048,128]{1,0:T(8,128)(2,1)}, u32[]{:S(2)}) %copy-start) | copy-done | bytes 524312
  49.5 0.0 copy-start.1
  49.5 1.0 %copy-done.1 = bf16[2048,128]{1,0:T(8,128)(2,1)S(1)} copy-done((bf16[2048,128]{1,0:T(8,128)(2,1)S(1)}, bf16[2048,128]{1,0:T(8,128)(2,1)}, u32[]{:S(2)}) %copy-start.1) | copy-done | bytes 524312
  50.6 0.0 copy-start.2
  50.6 0.9 %copy-done.2 = f32[2,256,128]{2,1,0:T(8,128)S(1)} copy-done((f32[2,256,128]{2,1,0:T(8,128)S(1)}, f32[2,256,128]{2,1,0:T(8,128)}, u32[]{:S(2)}) %copy-start.2) | copy-done | bytes 262168
  51.5 0.0 copy-start.3
  51.5 0.9 %copy-done.3 = f32[2,256,128]{2,1,0:T(8,128)S(1)} copy-done((f32[2,256,128]{2,1,0:T(8,128)S(1)}, f32[2,256,128]{2,1,0:T(8,128)}, u32[]{:S(2)}) %copy-start.3) | copy-done | bytes 262168
  52.5 0.0 copy-start.4
  52.5 0.7 %copy-done.4 = f32[8,2,256]{2,1,0:T(2,128)S(1)} copy-done((f32[8,2,256]{2,1,0:T(2,128)S(1)}, f32[8,2,256]{2,1,0:T(2,128)}, u32[]{:S(2)}) %copy-start.4) | copy-done | bytes 16408
  53.2 1.4 %shard_map.153 = (bf16[2048,128]{1,0:T(8,128)(2,1)}, bf16[2048,128]{1,0:T(8,128)(2,1)}, bf16[256,2,128]{2,1,0:T(2,128)(2,1)}, bf16[256,2,128]{2,1,0:T(2,128)(2,1...) custom-call(bf16[2048,128]{1,0:T(8,128)(2,1)S(1)} %copy-done, ...), custom_call_target="tpu_custom_call" | custom-call | tf_op jit(solution)/shard_map/pallas_call | solution.py:511
Async XLA Ops:
  47.8 0.7 %copy-start.5 = (f32[3,2,8]{2,1,0:T(2,128)S(1)}, f32[3,2,8]{2,1,0:T(2,128)}, u32[]{:S(2)}) copy-start(f32[3,2,8]{2,1,0:T(2,128)} %get-tuple-element.27.small) | copy-start | bytes 580
  48.5 1.0 %copy-start = (bf16[2048,128]{1,0:T(8,128)(2,1)S(1)}, bf16[2048,128]{1,0:T(8,128)(2,1)}, u32[]{:S(2)}) copy-start(bf16[2048,128]{1,0:T(8,128)(2,1)} %get-tuple-element.22.y) | copy-start | bytes 1572868
  49.5 1.0 %copy-start.1 = (bf16[2048,128]{1,0:T(8,128)(2,1)S(1)}, bf16[2048,128]{1,0:T(8,128)(2,1)}, u32[]{:S(2)}) copy-start(bf16[2048,128]{1,0:T(8,128)(2,1)} %get-tuple-element.23.dx) | copy-start | bytes 1572868
  50.6 0.9 %copy-start.2 = (f32[2,256,128]{2,1,0:T(8,128)S(1)}, f32[2,256,128]{2,1,0:T(8,128)}, u32[]{:S(2)}) copy-start(f32[2,256,128]{2,1,0:T(8,128)} %get-tuple-element.24.db) | copy-start | bytes 786436
  51.5 0.9 %copy-start.3 = (f32[2,256,128]{2,1,0:T(8,128)S(1)}, f32[2,256,128]{2,1,0:T(8,128)}, u32[]{:S(2)}) copy-start(f32[2,256,128]{2,1,0:T(8,128)} %get-tuple-element.25.dc) | copy-start | bytes 786436
  52.5 0.7 %copy-start.4 = (f32[8,2,256]{2,1,0:T(2,128)S(1)}, f32[8,2,256]{2,1,0:T(2,128)}, u32[]{:S(2)}) copy-start(f32[8,2,256]{2,1,0:T(2,128)} %get-tuple-element.26.step) | copy-start | bytes 49156

commit v3 on v2

--- a/solution.py
+++ b/solution.py
@@ -62,7 +62,7 @@
     x_ref, b_ref, c_ref, dy_ref, raw_ref, doc_ref, rate_ref, bias_ref, skip_ref,
     y_out, dx_out, db_out, dc_out, step_out, small_out,
     pars, gains,
-    wide, xg, bg, cg, gg, bt, ct, gt, tab, mask, prow,
+    wide, wb, wc, wd, xg, bg, cg, gg, bt, ct, gt, tab, mask, prow,
     loc_f, loc_b, s_in, s_out, d_out, d_in,
     ybuf, dxbuf, part, rows_r, rows_k, zrow, skiprow,
     xbuf, rbuf, sbuf,
@@ -100,19 +100,6 @@
             device_id={"seq": to // ndp, "dp": lax.rem(to, ndp)},
             device_id_type=MESH,
         )
-
-    for src, dst in ((x_ref, xg), (b_ref, bg), (c_ref, cg), (dy_ref, gg)):
-        width = src.shape[1]
-        wide[:, :width] = src[...].astype(F32)
-        for g in range(G):
-            block = wide[pl.ds(g, L, stride=G), :width]
-            dst[g] = block.astype(BF16)
-            if dst is bg:
-                bt[g] = block.T.astype(BF16)
-            if dst is cg:
-                ct[g] = block.T.astype(BF16)
-            if dst is gg:
-                gt[g] = block.T.astype(BF16)
 
     i0 = lax.broadcasted_iota(jnp.int32, (L, L), 0)
     i1 = lax.broadcasted_iota(jnp.int32, (L, L), 1)
@@ -194,14 +181,26 @@
     def mine_x(g):
         return g // (gl * fan) == me_x
 
+    stages = ((x_ref, wide, xg, None), (b_ref, wb, bg, bt), (c_ref, wc, cg, ct), (dy_ref, wd, gg, gt))
+    for src, buf, _, _ in stages:
+        buf[:, : src.shape[1]] = src[...].astype(F32)
     pl.semaphore_wait(barrier, (nmp - 1) + (npar - 1))
 
     @pl.loop(0, G)
     def _(p):
         g = at(p)
         cols = tab[g].T
-        loc_f[g] = right2(bt[g], xg[g].astype(F32) * spread(cols, 2 * H))
-        loc_b[g] = right2(ct[g], gg[g].astype(F32) * spread(cols, 3 * H))
+        for src, buf, dst, turned_dst in stages:
+            block = buf[pl.ds(g, L, stride=G), : src.shape[1]]
+            dst[g] = block.astype(BF16)
+            if turned_dst is not None:
+                turned_dst[g] = block.T.astype(BF16)
+            if src is x_ref:
+                xw = block * spread(cols, 2 * H)
+            if src is dy_ref:
+                gw = block * spread(cols, 3 * H)
+        loc_f[g] = right2(bt[g], xw)
+        loc_b[g] = right2(ct[g], gw)
 
         @pl.when(me_s == 0)
         def _():
@@ -296,11 +295,12 @@
                 def _():
                     send_m(g).start()
 
-    lag_f = me_s - 1
-    lag_b = last - me_s - 1
+    hop = 3
+    lag_f = (me_s - 1) * hop
+    lag_b = (last - me_s - 1) * hop
     lag = jnp.maximum(jnp.maximum(lag_f, lag_b), 0)
 
-    @pl.loop(0, G + max(nseq - 2, 0) + 1)
+    @pl.loop(0, G + hop * max(nseq - 2, 0) + 1)
     def _(i):
         @pl.when(i < G)
         def _():
@@ -473,7 +473,7 @@
     dma = pltpu.SemaphoreType.DMA
     scratch = [
         vm((npr, 128), F32), vm((G, hp), F32),
-        vm((L * G, max(hp, N)), F32),
+        vm((L * G, hp), F32), vm((L * G, N), F32), vm((L * G, N), F32), vm((L * G, hp), F32),
         vm((G, L, hp), BF16), vm((G, L, N), BF16), vm((G, L, N), BF16), vm((G, L, hp), BF16),
         vm((G, N, L), BF16), vm((G, N, L), BF16), vm((G, hp, L), BF16),
         vm((G, nr, L), F32), vm((L, L), F32), vm((G, 1, hp), F32),
@@ -522,7 +522,7 @@
         ),
         in_specs=[pl.BlockSpec(memory_space=pltpu.VMEM)] * 6,
         out_specs=[pl.BlockSpec(memory_space=pltpu.VMEM)] * 8,
-        compiler_params=pltpu.CompilerParams(vmem_limit_bytes=32 * 2**20),
+        compiler_params=pltpu.CompilerParams(vmem_limit_bytes=60 * 2**20),
     )(*made)
     return (
         y.reshape(1, L, G, hp),

time: 55 us -> 42.5 us (0.77)
  Pallas kernels: 48.6 us -> 41.7 us
  local copies, waits for them, and re-layouts: 5.37 us -> 0 us
    pallas_call x1, Pallas kernels: 47.2 us -> 39.2 us  [local(): pl.pallas_call(functools.partial(kernel, nseq, ndp, nmp, L, G, H, N), out...]
    unnamed x12 -> x0, local copies, waits for them, and re-layouts: 5.37 us -> none
    pallas_call x1, Pallas kernels: 1.42 us -> 2.49 us  [local(): pl.pallas_call(leave, out_shape=(jax.ShapeDtypeStruct((L * G, hp), BF16),...]
where the time goes in v3:
time: 42.5 us; the launch traced here: 42.3 us
  Pallas kernels  41.7 us (98%)
  between operations  0.64 us (2%)
    pallas_call x1, Pallas kernels, local(): pl.pallas_call(functools.partial(kernel, nseq, ndp, nmp, L, G, H, N), out...  39.2 us
    pallas_call x1, Pallas kernels, local(): pl.pallas_call(leave, out_shape=(jax.ShapeDtypeStruct((L * G, hp), BF16),...  2.49 us

profile of v3, /device:TPU:1, one launch (start us, length us, event | category | flops | bytes accessed | tf_op | source)
XLA Modules:
  0.0 42.3 jit_solution(15711689501678132013)
XLA Ops:
  0.6 39.2 %shard_map.152 = (bf16[2048,128]{1,0:T(8,128)(2,1)}, bf16[2048,128]{1,0:T(8,128)(2,1)}, f32[2,256,128]{2,1,0:T(8,128)}, f32[2,256,128]{2,1,0:T(8,128)}, f32[8,2,256]{2,1,0:T(2,128)}, /*index=5*/f32[3,2,8]{2,1,0:T(2,128)}) custom-call(bf16[2048,128]{1,0:T(8,128)(2,1)} %bitcast.20, bf16[2048,128]{1,0:T(8,128)(2,1)} %bitcast.21, bf16[2048,128]{1,0:T(8,128)(2,1)} %bitcast.22, ...), custom_call_target="tpu_custom_call" | custom-call | tf_op jit(solution)/shard_map/pallas_call | solution.py:488
  39.8 2.5 %shard_map.153 = (bf16[2048,128]{1,0:T(8,128)(2,1)}, bf16[2048,128]{1,0:T(8,128)(2,1)}, bf16[256,2,128]{2,1,0:T(2,128)(2,1)}, bf16[256,2,128]{2,1,0:T(2,128)(2,1...) custom-call(bf16[2048,128]{1,0:T(8,128)(2,1)} %get-tuple-element.22.y, ...), custom_call_target="tpu_custom_call" | custom-call | tf_op jit(solution)/shard_map/pallas_call | solution.py:511

commit v4 on v3

--- a/solution.py
+++ b/solution.py
@@ -224,8 +224,11 @@
         grad_s = None
         y = None
         dxt = []
-        pr = jnp.zeros((8, L), F32)
-        head_row = lax.broadcasted_iota(jnp.int32, (8, 128), 0)
+        folds = []
+        pick = lax.broadcasted_iota(jnp.int32, (8, 128 * H), 0) == (
+            lax.broadcasted_iota(jnp.int32, (8, 128 * H), 1) // 128
+        )
+        pick = jnp.where(pick, 1.0, 0.0).astype(BF16)
         for h in range(H):
             xm = jnp.where(lanes_l == h, xb.astype(F32), 0.0).astype(BF16)
             dm = mm(gb, xm, NT)
@@ -239,22 +242,21 @@
             folded = q[:, 0:128]
             for j in range(128, L, 128):
                 folded = folded + q[:, j : j + 128]
-            pick = jnp.where(head_row == h, 1.0, 0.0).astype(BF16)
-            pr = pr + right3(pick, folded, NT)
+            folds.append(folded)
             hi, lo = split2(mix)
             now = mm(hi, xm) + mm(lo, xm)
             y = now if y is None else y + now
             gth = gt[g, h * P_SIZE : (h + 1) * P_SIZE, :]
             dxt.append(mm(gth, hi) + mm(gth, lo))
-        rows_r[g] = pr
+        rows_r[g] = right3(pick, folds[0] if H == 1 else jnp.concatenate(folds, axis=1), NT)
         ybuf[g] = y
         dxbuf[g] = (dxt[0] if H == 1 else jnp.concatenate(dxt, axis=0)).T
         hi, lo = split2(grad_s)
         part[g, 1] = mm(hi, bb) + mm(lo, bb)
         part[g, 0] = (mm(ct[g], hi) + mm(ct[g], lo)).T
 
-    head8 = lax.broadcasted_iota(jnp.int32, (8, hp), 0)
-    sel = jnp.where(head8 == lax.broadcasted_iota(jnp.int32, (8, hp), 1) // P_SIZE, 1.0, 0.0)
+    head8 = lax.broadcasted_iota(jnp.int32, (8, 2 * hp), 0)
+    sel = jnp.where(head8 == lax.broadcasted_iota(jnp.int32, (8, 2 * hp), 1) // P_SIZE, 1.0, 0.0)
     sel = sel.astype(BF16)
 
     def finish(g):
@@ -268,10 +270,9 @@
         dxo = right2(bb, dso) * wl
         ybuf[g] = ybuf[g] + yo + gain * xf
         dxbuf[g] = dxbuf[g] + dxo + gain * gf
-        e_rows = right3(sel, gf * yo, NT)
-        f_rows = right3(sel, xf * dxo, NT)
-        rows_r[g] = rows_r[g] + e_rows
-        rows_k[g, 0:H, :] = rows_k[g, 0:H, :] + f_rows[0:H]
+        ef = right3(sel, jnp.concatenate([gf * yo, xf * dxo], axis=1), NT)
+        rows_r[g, 0:H, :] = rows_r[g, 0:H, :] + ef[0:H]
+        rows_k[g, 0:H, :] = rows_k[g, 0:H, :] + ef[H : 2 * H]
         part[g, 1] = part[g, 1] + both2(gf * el, sin, NT)
         part[g, 0] = part[g, 0] + both2(xf * wl, dso, NT)
         skiprow[g] = jnp.sum(gf * xf, axis=0, keepdims=True)

time: 42.5 us -> 41.9 us (0.986)
  Pallas kernels: 41.7 us -> 41.1 us
    pallas_call x1, Pallas kernels: 39.2 us -> 38.6 us  [local(): pl.pallas_call(functools.partial(kernel, nseq, ndp, nmp, L, G, H, N), out...]
where the time goes in v4:
time: 41.9 us; the launch traced here: 41.7 us
  Pallas kernels  41.1 us (98%)
  between operations  0.64 us (2%)
    pallas_call x1, Pallas kernels, local(): pl.pallas_call(functools.partial(kernel, nseq, ndp, nmp, L, G, H, N), out...  38.6 us
    pallas_call x1, Pallas kernels, local(): pl.pallas_call(leave, out_shape=(jax.ShapeDtypeStruct((L * G, hp), BF16),...  2.49 us

profile of v4, /device:TPU:1, one launch (start us, length us, event | category | flops | bytes accessed | tf_op | source)
XLA Modules:
  0.0 41.7 jit_solution(8008178686245655430)
XLA Ops:
  0.6 38.6 %shard_map.152 = (bf16[2048,128]{1,0:T(8,128)(2,1)}, bf16[2048,128]{1,0:T(8,128)(2,1)}, f32[2,256,128]{2,1,0:T(8,128)}, f32[2,256,128]{2,1,0:T(8,128)}, f32[8,2,256]{2,1,0:T(2,128)}, /*index=5*/f32[3,2,8]{2,1,0:T(2,128)}) custom-call(bf16[2048,128]{1,0:T(8,128)(2,1)} %bitcast.20, bf16[2048,128]{1,0:T(8,128)(2,1)} %bitcast.21, bf16[2048,128]{1,0:T(8,128)(2,1)} %bitcast.22, ...), custom_call_target="tpu_custom_call" | custom-call | tf_op jit(solution)/shard_map/pallas_call | solution.py:489
  39.2 2.5 %shard_map.153 = (bf16[2048,128]{1,0:T(8,128)(2,1)}, bf16[2048,128]{1,0:T(8,128)(2,1)}, bf16[256,2,128]{2,1,0:T(2,128)(2,1)}, bf16[256,2,128]{2,1,0:T(2,128)(2,1...) custom-call(bf16[2048,128]{1,0:T(8,128)(2,1)} %get-tuple-element.22.y, ...), custom_call_target="tpu_custom_call" | custom-call | tf_op jit(solution)/shard_map/pallas_call | solution.py:512
